TPU v7x, 128 devices: a whole 4x4x4 slice. The times are simulated.
128 devices in a mesh: fsdp: 32 (over x, y, core), ctx: 4 (over z).
Axes of the slice: x: 4, y: 4, z: 4, core: 2. Of those that a mesh axis runs over, the one named last changes fastest.
Arguments:
- tokens: bfloat16 [64, 512, 768], P('fsdp', 'ctx'), may hold values from -6 to 6
- cotangent: bfloat16 [64, 512, 768], P('fsdp', 'ctx'), may hold values from -6 to 6
- lengths: int32 [64, 4], P('fsdp'), may hold values from 0 to 512, as said below
- input_weight: float32 [768, 2304], P('fsdp'), may hold values from -0.21875 to 0.21875
- output_weight: float32 [768, 768], P('fsdp'), may hold values from -0.4375 to 0.4375
- expand_weight: float32 [768, 3072], P('fsdp'), may hold values from -0.21875 to 0.21875
- shrink_weight: float32 [3072, 768], P('fsdp'), may hold values from -0.109375 to 0.109375
- vectors: float32 [768, 8], P('fsdp'), may hold values from -1.2 to 1.3
- expand_bias: float32 [3072], P('fsdp'), may hold values from -1.2 to 1.2
- input_moment: float32 [768, 2304], P('fsdp'), may hold values from -40.18629 to 40.18629
- output_moment: float32 [768, 768], P('fsdp'), may hold values from -40.18629 to 40.18629
- expand_moment: float32 [768, 3072], P('fsdp'), may hold values from -40.18629 to 40.18629
- shrink_moment: float32 [3072, 768], P('fsdp'), may hold values from -40.18629 to 40.18629
- vectors_moment: float32 [768, 8], P('fsdp'), may hold values from -80.372585 to 80.372585
- biases_moment: float32 [3072], P('fsdp'), may hold values from -40.18629 to 40.18629
- input_square: float32 [768, 2304], P('fsdp'), may hold values from 8.192 to 32.768
- output_square: float32 [768, 768], P('fsdp'), may hold values from 8.192 to 32.768
- expand_square: float32 [768, 3072], P('fsdp'), may hold values from 8.192 to 32.768
- shrink_square: float32 [3072, 768], P('fsdp'), may hold values from 8.192 to 32.768
- vectors_square: float32 [768, 8], P('fsdp'), may hold values from 32.768 to 131.072
- biases_square: float32 [3072], P('fsdp'), may hold values from 8.192 to 32.768
Outputs:
- layer_output: bfloat16 [64, 512, 768], P('fsdp', 'ctx')
- tokens_gradient: float32 [64, 512, 768], P('fsdp', 'ctx')
- updated_input: float32 [768, 2304], P('fsdp')
- updated_output: float32 [768, 768], P('fsdp')
- updated_expand: float32 [768, 3072], P('fsdp')
- updated_shrink: float32 [3072, 768], P('fsdp')
- updated_vectors: float32 [768, 8], P('fsdp')
- updated_biases: float32 [3072], P('fsdp')
- average_input: float32 [768, 2304], P('fsdp')
- average_output: float32 [768, 768], P('fsdp')
- average_expand: float32 [768, 3072], P('fsdp')
- average_shrink: float32 [3072, 768], P('fsdp')
- average_vectors: float32 [768, 8], P('fsdp')
- average_biases: float32 [3072], P('fsdp')
- squares_input: float32 [768, 2304], P('fsdp')
- squares_output: float32 [768, 768], P('fsdp')
- squares_expand: float32 [768, 3072], P('fsdp')
- squares_shrink: float32 [3072, 768], P('fsdp')
- squares_vectors: float32 [768, 8], P('fsdp')
- squares_biases: float32 [3072], P('fsdp')
Inputs may be any that keep to these rules, and one draw needn't show every extreme that they name: Row g holds the lengths of the sequences packed in that order from position 0 of pack g; the positions after them up to 512 are padding, a multiple of 128 and fewer than 128; some sequence of every row starts within the first 128 positions and ends within the last 128; some row is a single sequence of 512.
All inputs are finite; a program needn't handle non-finite values.
Results may differ from a plain program's by a relative error of at most 0.025.
Values may be sent and summed in bfloat16 or wider, within the bound.
A program may use at most 128 MiB of HBM per device.

v0:
```python
import jax, jax.numpy as jnp
from jax import lax
from jax.experimental import pallas as pl
from jax.experimental.pallas import tpu as pltpu
from jax.sharding import PartitionSpec as P

MESH = pl.DeviceIdType.MESH
BF = jnp.bfloat16
F32 = jnp.float32


def flip1(v):
    return v + 1 - 2 * (v % 2)


class Links:
    def __init__(self, send_sems, recv_sems):
        self.send_sems, self.recv_sems, self.used = send_sems, recv_sems, 0
        me = lax.axis_index("fsdp")
        self.z = lax.axis_index("ctx")
        self.core = me % 2
        self.chip = me // 2
        self.x, self.y = self.chip // 4, self.chip % 4
        self.sib = {"fsdp": me + 1 - 2 * self.core}
        self.pending = []

    def at(self, axis, kind):
        v = {"x": self.x, "y": self.y, "z": self.z}[axis]
        return flip1(v) if kind == 1 else 3 - v

    def dev(self, axis, kind):
        if axis == "z":
            return {"ctx": self.at("z", kind)}
        x = self.at("x", kind) if axis == "x" else self.x
        y = self.at("y", kind) if axis == "y" else self.y
        return {"fsdp": (x * 4 + y) * 2 + self.core}

    def send(self, src, dst, device):
        i = self.used
        self.used += 1
        copy = pltpu.make_async_remote_copy(
            src_ref=src, dst_ref=dst, send_sem=self.send_sems.at[i],
            recv_sem=self.recv_sems.at[i], device_id=device, device_id_type=MESH,
        )
        copy.start()
        self.pending.append(copy)
        return copy

    def barrier(self, devices):
        sem = pltpu.get_barrier_semaphore()
        for d in devices:
            pl.semaphore_signal(sem, inc=1, device_id=d, device_id_type=MESH)
        pl.semaphore_wait(sem, len(devices))

    def sent(self, copy):
        copy.wait_send()
        self.pending = [q for q in self.pending if q is not copy]

    def drain(self):
        for c in self.pending:
            c.wait_send()
        self.pending = []


ORDERS = (
    (("y", 1), ("y", 3), ("x", 1), ("x", 3)),
    (("y", 3), ("y", 1), ("x", 3), ("x", 1)),
    (("x", 1), ("x", 3), ("y", 1), ("y", 3)),
    (("x", 3), ("x", 1), ("y", 3), ("y", 1)),
)


def held(v, kind, count):
    if count == 0:
        return [(v, 1)]
    if count == 2:
        return [(0, 4)]
    if kind == 1:
        return [(v - v % 2, 2)]
    return [(v, 1), (3 - v, 1)]


def regions(links, flavor, step, coords):
    order = ORDERS[flavor]
    first, second = order[0][0], order[2][0]
    a = held(coords[first], order[0][1], min(step, 2))
    b = held(coords[second], order[2][1], max(step - 2, 0))
    out = []
    for i, (sa, na) in enumerate(a):
        for j, (sb, nb) in enumerate(b):
            sel = {first: pl.ds(sa, na), second: pl.ds(sb, nb)}
            out.append((sel["x"], sel["y"], i, j, {first: na, second: nb}))
    return out


def gather_step(links, pieces, step):
    copies = []
    for flavor, view in pieces:
        axis, kind = ORDERS[flavor][step]
        device = links.dev(axis, kind)
        for xs, ys, *_ in regions(links, flavor, step, {"x": links.x, "y": links.y}):
            copies.append(links.send(view(xs, ys), view(xs, ys), device))
    return copies


def pair_of(v, kind):
    if kind == 1:
        return [v - v % 2, v - v % 2 + 1]
    return [v, 3 - v]


class Scatter:
    def __init__(self, links, pieces, bufs):
        self.links, self.pieces, self.bufs = links, pieces, bufs

    def _sel(self, flavor, a, b):
        first = ORDERS[flavor][0][0]
        return (a, b) if first == "x" else (b, a)

    def start(self, step):
        L = self.links
        self.copies = []
        for flavor, acc, sub in self.pieces:
            order = ORDERS[flavor]
            axis, kind = order[3 - step]
            first, second = order[0][0], order[2][0]
            va, vb = {"x": L.x, "y": L.y}[first], {"x": L.x, "y": L.y}[second]
            p = L.at(axis, kind)
            dev = L.dev(axis, kind)
            if step == 0:
                for j, b in enumerate(pair_of(p, order[2][1])):
                    self.copies.append(L.send(acc(*self._sel(flavor, pl.ds(0, 4), b)), sub(self.bufs[0].at[j]), dev))
            elif step == 1:
                self.copies.append(L.send(acc(*self._sel(flavor, pl.ds(0, 4), p)), sub(self.bufs[1]), dev))
            elif step == 2:
                for j, a in enumerate(pair_of(p, order[0][1])):
                    self.copies.append(L.send(acc(*self._sel(flavor, a, vb)), sub(self.bufs[2].at[j]), dev))
            else:
                self.copies.append(L.send(acc(*self._sel(flavor, p, vb)), sub(self.bufs[3]), dev))

    def finish(self, step):
        L = self.links
        for c in self.copies:
            c.wait_recv()

        def add(view, buf):
            view[...] = (view[...].astype(F32) + buf[...].astype(F32)).astype(BF)

        for flavor, acc, sub in self.pieces:
            order = ORDERS[flavor]
            first, second = order[0][0], order[2][0]
            va, vb = {"x": L.x, "y": L.y}[first], {"x": L.x, "y": L.y}[second]
            if step == 0:
                for j, b in enumerate(pair_of(vb, order[2][1])):
                    for a in range(4):
                        add(acc(*self._sel(flavor, a, b)), sub(self.bufs[0].at[j, a]))
            elif step == 1:
                for a in range(4):
                    add(acc(*self._sel(flavor, a, vb)), sub(self.bufs[1].at[a]))
            elif step == 2:
                for j, a in enumerate(pair_of(va, order[0][1])):
                    add(acc(*self._sel(flavor, a, vb)), sub(self.bufs[2].at[j]))
            else:
                add(acc(*self._sel(flavor, va, vb)), sub(self.bufs[3]))


def lanes(n, size):
    return lambda ref: ref.at[..., pl.ds(n, size)]


def rows(n, size):
    return lambda ref: ref.at[..., pl.ds(n, size), :]


PIECES = (
    tuple((f, lanes(f * 128, 128)) for f in range(3)) + ((3, lanes(384, 384)),),
    tuple((f, lanes(f * 384, 384)) for f in range(4)),
    tuple((f, rows(f * 48, 48)) for f in range(4)),
)


D = 768
H = 12
HD = 64
FF = 3072
STEP = 10


norm_eps = 1e-05
beta_first = 0.9
beta_second = 0.999
adam_eps = 1e-08
decay_rate = 0.01


def adam_step(weight, gradient, moment, square, rate):
    moment_new = beta_first * moment + (1.0 - beta_first) * gradient
    square_new = beta_second * square + (1.0 - beta_second) * gradient * gradient
    corrected = moment_new / (1.0 - beta_first**STEP)
    spread = jnp.sqrt(square_new / (1.0 - beta_second**STEP)) + adam_eps
    return (weight - rate * (corrected / spread + decay_rate * weight), moment_new, square_new)


NN = ((1,), (0,))
NT = ((1,), (1,))
TN = ((0,), (0,))


def dot(a, b, dims):
    return lax.dot_general(a, b, (dims, ((), ())), preferred_element_type=F32)


def norm_stats(v):
    center = v - jnp.mean(v, -1, keepdims=True)
    r = lax.rsqrt(jnp.mean(center * center, -1, keepdims=True) + norm_eps)
    return center * r, r


def norm_back(z, xhat, r, g):
    zg = z * g
    return r * (zg - jnp.mean(zg, -1, keepdims=True) - xhat * jnp.mean(zg * xhat, -1, keepdims=True))


def colsum(v):
    return jnp.sum(v, 0, keepdims=True)


SHAPES = ((48, 768), (48, 1536), (192, 384))


def layer_kernel(
    lengths, tok_hbm, tok, cot, win, wout, wexp, wshr, sm,
    out, tgrad, o0, oi, o1, o2, osm,
    f0a, f0b, f1, f2, sbuf, gbuf,
    G0, G1, G2, A0, A1, A2, S0, S1, S2,
    R00, R01, R02, R03, R10, R11, R12, R13, R20, R21, R22, R23,
    zi, z0, z1, z2, fi, f0f, f1f, f2f,
    X, QK, V, P, MB, CS, CT, after, xh2, r2, second, sect, hidden, slope, up, ab, CBS, CB, PQK, PV, N1, N2,
    ss, rs, ls,
):
    L = Links(ss, rs)
    c, z, x, y = L.core, L.z, L.x, L.y
    me = {"x": x, "y": y}
    zf, zt, zo = L.at("z", 1), L.at("z", 3), (z + 2) % 4
    zpeers = (zf, zt, zo)
    L.barrier([L.sib] + [L.dev(a, k) for a in "xyz" for k in (1, 3)] + [{"ctx": zo}])
    G, A, S = [G0, G1, G2], [A0, A1, A2], [S0, S1, S2]

    def wait(copies):
        for q in copies:
            q.wait_recv()

    local = [0]

    def move(src, dst):
        cp = pltpu.make_async_copy(src, dst, ls.at[local[0]])
        local[0] += 1
        cp.start()
        return cp

    stages = [L.sib] + [L.dev(a, k) for a, k in (("y", 1), ("y", 3), ("x", 1), ("x", 3), ("z", 1), ("z", 3))]

    class Sum:
        def __init__(self, buf):
            self.buf = buf

        def start(self, i):
            self.copy = L.send(self.buf.at[0], self.buf.at[i + 1], stages[i])

        def finish(self, i):
            self.copy.wait_recv()
            L.sent(self.copy)
            self.buf[0] = self.buf[0] + self.buf[i + 1]

    small = Sum(sbuf)
    sbuf[0] = sm[...]
    small.start(0)

    def halves(src, n, dst, nr):
        other, mine = pl.multiple_of((1 - c) * n, 128), pl.multiple_of(c * n, 128)
        r = pl.ds(pl.multiple_of(nr * c, 8), nr)
        return L.send(src.at[:, pl.ds(other, n)], dst.at[r], L.sib), move(src.at[:, pl.ds(mine, n)], dst.at[r])

    pairs = [halves(win, 384, f0a, 24), halves(wout, 384, f0b, 24)]
    xl = move(tok_hbm, X.at[:, z])
    tz = []
    for p in range(2):
        for h, k in enumerate((1, 3)):
            r = pl.ds(h * 64, 64)
            tz.append(L.send(tok_hbm.at[p, r], X.at[p, z, r], L.dev("z", k)))
    pairs += [halves(wexp, 1536, f1, 24), halves(wshr, 384, f2, 96)]

    views = []
    for g in range(3):
        views.append([(f, (lambda sub, g: lambda xs, ys: sub(G[g].at[c, xs, ys]))(sub, g)) for f, sub in PIECES[g]])
    flight = {}

    def start(g, s):
        flight[g] = gather_step(L, views[g], s)

    def advance(g, s):
        wait(flight[g])
        start(g, s)

    def to_sibling(g, arrived):
        res = []
        for f, view in views[g]:
            axis, kind = ORDERS[f][3]
            o = dict(me)
            if arrived:
                o[axis] = L.at(axis, kind)
            for xs, ys, *_ in regions(L, f, 3, o):
                res.append(L.send(view(xs, ys), view(xs, ys), L.sib))
        return res

    for cp, lc in pairs[:2]:
        cp.wait_recv()
        lc.wait()
    G0[c, x, y, :, 0:384] = f0a[...].astype(BF)
    G0[c, x, y, :, 384:768] = f0b[...].astype(BF)
    start(0, 0)
    small.finish(0)
    small.start(1)
    for g, f in ((1, f1), (2, f2)):
        cp, lc = pairs[g + 1]
        cp.wait_recv()
        lc.wait()
        G[g][c, x, y] = f[...].astype(BF)
        start(g, 0)
    advance(0, 1)
    small.finish(1)
    small.start(2)
    xl.wait()
    tz2 = []
    for p in range(2):
        for h, (k1, k2) in enumerate(((1, 3), (3, 1))):
            r = pl.ds(h * 64, 64)
            tz[2 * p + h].wait_recv()
            q = L.at("z", k1)
            tz2.append([L.send(X.at[p, b, r], X.at[p, b, r], L.dev("z", k2)) for b in (z, q)])
    advance(0, 2)
    small.finish(2)
    small.start(3)
    advance(1, 1)
    advance(2, 1)
    advance(0, 3)
    sib = {0: to_sibling(0, False)}
    small.finish(3)
    small.start(4)

    seqs = lengths.shape[1]

    def segment(p, shape, dim):
        pos = lax.broadcasted_iota(jnp.int32, shape, dim)
        end = lengths[p, 0]
        seg = (pos >= end).astype(jnp.int32)
        for i in range(1, seqs):
            end = end + lengths[p, i]
            seg = seg + (pos >= end).astype(jnp.int32)
        return seg

    def fill_mask(p):
        ok = segment(p, (512, 1), 0) == segment(p, (1, 512), 1)
        ok = ok & (lax.broadcasted_iota(jnp.int32, (512, 512), 1) <= lax.broadcasted_iota(jnp.int32, (512, 512), 0))
        MB[...] = jnp.where(ok, 0.0, -1e30)

    def live_rows(p):
        pos = lax.broadcasted_iota(jnp.int32, (128, 1), 0) + z * 128
        total = lengths[p, 0]
        for i in range(1, seqs):
            total = total + lengths[p, i]
        return (pos < total).astype(F32)

    small.finish(4)
    g1, b1 = sbuf[0, 0:1], sbuf[0, 1:2]

    def ready(p):
        for q in tz2[2 * p] + tz2[2 * p + 1]:
            q.wait_recv()
            L.sent(q)

    def project(p):
        for b in range(4):
            xhat, _ = norm_stats(X[p, b].astype(F32))
            X[p, b] = (xhat * g1 + b1).astype(BF)

    def qkv(p):
        n = X[p].reshape(512, 768)
        qk = dot(n, G0[0, :, :, :, 0:384].reshape(768, 384), NN)
        q = (qk[:, 0:192] + sbuf[0, 12:13, 0:192]) * 0.125
        QK[p] = jnp.concatenate([q, qk[:, 192:384]], 1).astype(BF)
        V[p] = (dot(n, G0[1, :, :, :, 0:256].reshape(768, 256), NN) + sbuf[0, 13:14, 0:256]).astype(BF)

    def attend(p):
        parts = [[], []]
        for h in range(3):
            q = QK[p, :, h * 64 : h * 64 + 64]
            k = QK[p, :, 192 + h * 64 : 256 + h * 64]
            v = V[p, :, h * 64 : h * 64 + 64]
            for i in range(2):
                r, n = i * 256, (i + 1) * 256
                s = dot(q[r : r + 256], k[:n], NT) + MB[r : r + 256, 0:n]
                e = jnp.exp(s - jnp.max(s, -1, keepdims=True))
                pr = (e * (1.0 / jnp.sum(e, -1, keepdims=True))).astype(BF)
                P[p * 3 + h, r : r + 256, 0:n] = pr
                parts[i].append(dot(pr, v[:n], NN))
        for i in range(2):
            ctx = jnp.concatenate(parts[i], 1).astype(BF)
            CS[p, 2 * i : 2 * i + 2] = ctx.reshape(2, 128, 192)

    def to_heads_owner(p, src, dst):
        res = [L.send(src.at[p, q], dst.at[z, p], {"ctx": q}) for q in zpeers]
        return res

    ready(0)
    project(0)
    wait(flight[0])
    sib[0] += to_sibling(0, True)
    advance(1, 2)
    advance(2, 2)
    fill_mask(0)
    wait(sib[0])
    qkv(0)
    attend(0)
    ctx_moves = to_heads_owner(0, CS, CT)
    own = [move(CS.at[0, z], CT.at[z, 0])]
    advance(1, 3)
    sib[1] = to_sibling(1, False)
    advance(2, 3)
    sib[2] = to_sibling(2, False)
    ready(1)
    project(1)
    fill_mask(1)
    qkv(1)
    attend(1)
    ctx_moves += to_heads_owner(1, CS, CT)
    own.append(move(CS.at[1, z], CT.at[z, 1]))
    wait(flight[1])
    sib[1] += to_sibling(1, True)
    wait(flight[2])
    sib[2] += to_sibling(2, True)
    for q in own:
        q.wait()
    wait(ctx_moves)

    bo, g2, b2, bd = sbuf[0, 4:5], sbuf[0, 5:6], sbuf[0, 6:7], sbuf[0, 7:8]
    for h in range(2):
        acc = sbuf[0, 4:5, h * 384 : h * 384 + 384] + tok[:, :, h * 384 : h * 384 + 384].astype(F32).reshape(256, 384)
        for q in range(4):
            acc = acc + dot(CT[q].reshape(256, 192), G0[h, q, :, :, 384:768].reshape(192, 384), NN)
        after[:, h * 384 : h * 384 + 384] = acc
    xhat, r = norm_stats(after[...])
    xh2[...] = xhat
    r2[...] = r
    sec = (xhat * g2 + b2).astype(BF)
    second[...] = sec
    sect[...] = sec.T
    live = [live_rows(p) for p in range(2)]
    for p in range(2):
        up[p * 128 : p * 128 + 128] = cot[p] * live[p].astype(BF)

    wait(sib[1])
    for t in range(4):
        lane = (t % 2) * 768
        e = dot(second[...], G1[t // 2, :, :, :, lane : lane + 768].reshape(768, 768), NN) + sbuf[0, 8 + t : 9 + t]
        cdf = 0.5 * (1.0 + lax.erf(e * (2.0 ** -0.5)))
        hidden[:, t * 768 : t * 768 + 768] = (e * cdf).astype(BF)
        slope[:, t * 768 : t * 768 + 768] = (cdf + e * (jnp.exp(-0.5 * e * e) * 0.3989422804014327)).astype(BF)
    wait(sib[2])

    for t in range(4):
        for h in range(2):
            d = dot(hidden[:, t * 768 : t * 768 + 768], up[:, h * 384 : h * 384 + 384], TN)
            A2[h, t] = d.astype(BF).reshape(4, 192, 384)

    def pieces_of(i):
        return [(f, (lambda sub: lambda xs, ys: sub(A[i].at[c, xs, ys]))(sub), sub) for f, sub in PIECES[i]]

    bufs = [[R00, R01, R02, R03], [R10, R11, R12, R13], [R20, R21, R22, R23]]
    sc = [Scatter(L, pieces_of(i), bufs[i]) for i in range(3)]
    pair = {}

    def pair_start(i):
        pair[i] = L.send(A[i].at[1 - c], S[i], L.sib)

    def pair_finish(i):
        pair[i].wait_recv()

        @pl.loop(0, 4)
        def _(k):
            A[i][c, k] = (A[i][c, k].astype(F32) + S[i][k].astype(F32)).astype(BF)

        sc[i].start(0)

    def turn(i, s):
        sc[i].finish(s)
        if s < 3:
            sc[i].start(s + 1)

    pair_start(2)

    for h in range(2):
        w = after[:, h * 384 : h * 384 + 384] + bd[:, h * 384 : h * 384 + 384]
        for t in range(4):
            w = w + dot(hidden[:, t * 768 : t * 768 + 768], G2[h, t].reshape(768, 384), NN)
        for p in range(2):
            out[p, :, h * 384 : h * 384 + 384] = (w[p * 128 : p * 128 + 128] * live[p]).astype(BF)
    pair_finish(2)

    resid = after
    gsum = Sum(gbuf)
    for t in range(4):
        lane = (t % 2) * 768
        cols = pl.ds(t * 768, 768)
        hb = dot(up[:, 0:384], G2[0, t].reshape(768, 384), NT) + dot(up[:, 384:768], G2[1, t].reshape(768, 384), NT)
        eb = (hb * slope[:, cols].astype(F32)).astype(BF)
        hidden[:, cols] = eb
        gbuf[0, 8 + t : 9 + t] = colsum(eb.astype(F32))
        part = dot(eb, G1[t // 2, :, :, :, lane : lane + 768].reshape(768, 768), NT)
        if t == 0:
            resid[...] = part
        else:
            resid[...] += part
        for q in range(4):
            d = dot(sect[q * 192 : q * 192 + 192], eb, NN).astype(BF)
            A1[t // 2, q, :, :, lane : lane + 768] = d.reshape(4, 48, 768)
    pair_start(1)
    turn(2, 0)
    sb = resid[...]
    gbuf[0, 5:6] = colsum(sb * xh2[...])
    gbuf[0, 6:7] = colsum(sb)
    up32 = up[...].astype(F32)
    gbuf[0, 7:8] = colsum(up32)
    res = up32 + norm_back(sb, xh2[...], r2[...], g2)
    resid[...] = res
    ab[...] = res.astype(BF)
    gbuf[0, 4:5] = colsum(ab[...].astype(F32))

    for q in range(4):
        d = dot(ab[:, 0:384], G0[0, q, :, :, 384:768].reshape(192, 384), NT)
        d = d + dot(ab[:, 384:768], G0[1, q, :, :, 384:768].reshape(192, 384), NT)
        CBS[:, q] = d.astype(BF).reshape(2, 128, 192)
    back_moves = [to_heads_owner(p, CBS, CB) for p in range(2)]
    own = [move(CBS.at[p, z], CB.at[z, p]) for p in range(2)]
    for q in range(4):
        d = dot(CT[q].reshape(256, 192), ab[...], TN).astype(BF)
        for h in range(2):
            A0[h, q, :, :, 384:768] = d[:, h * 384 : h * 384 + 384].reshape(4, 48, 384)
    pair_finish(1)
    turn(2, 1)

    def attend_back(p):
        co = CB[:, p].reshape(512, 192)
        dqs, dks, dvs = [[], []], [], []
        for h in range(3):
            do = co[:, h * 64 : h * 64 + 64]
            q = QK[p, :, h * 64 : h * 64 + 64]
            k = QK[p, :, 192 + h * 64 : 256 + h * 64]
            v = V[p, :, h * 64 : h * 64 + 64]
            dk, dv = [], []
            for i in range(2):
                r, n = i * 256, (i + 1) * 256
                pr = P[p * 3 + h, r : r + 256, 0:n]
                p32 = pr.astype(F32)
                dp = dot(do[r : r + 256], v[:n], NT)
                ds = (p32 * (dp - jnp.sum(p32 * dp, -1, keepdims=True))).astype(BF)
                dqs[i].append(dot(ds, k[:n], NN) * 0.125)
                dk.append(dot(ds, q[r : r + 256], TN))
                dv.append(dot(pr, do[r : r + 256], TN))
            dks.append([dk[0] + dk[1][:256], dk[1][256:]])
            dvs.append([dv[0] + dv[1][:256], dv[1][256:]])
        for i in range(2):
            r = i * 256
            PQK[p, r : r + 256] = jnp.concatenate(dqs[i] + [d[i] for d in dks], 1).astype(BF)
            PV[p, r : r + 256] = jnp.concatenate([d[i] for d in dvs] + [jnp.zeros((256, 64), F32)], 1).astype(BF)

    def NB(p, b):
        lane = b * 768 if isinstance(b, int) else pl.multiple_of(b * 768, 128)
        return hidden.at[pl.ds(p * 128, 128), pl.ds(lane, 768)]

    nb_moves = [None, None]
    kinds = ((1, 3), (3, 1))

    def inner_back(p):
        n = dot(PQK[p], G0[0, :, :, :, 0:384].reshape(768, 384), NT)
        n = n + dot(PV[p], G0[1, :, :, :, 0:256].reshape(768, 256), NT)
        for b in range(4):
            NB(p, b)[...] = n[b * 128 : b * 128 + 128].astype(BF)
        k1, k2 = kinds[p]
        q = L.at("z", k1)
        nb_moves[p] = [L.send(NB(p, b), N1.at[p, j], L.dev("z", k1)) for j, b in enumerate((q, zo if k2 != k1 else q))]

    for p in range(2):
        own[p].wait()
        wait(back_moves[p])
        attend_back(p)
        inner_back(p)
        turn(2, 2 + p)
        if p == 0:
            turn(1, 0)
    for q in range(2):
        xs, n = slice(2 * q, 2 * q + 2), X[:, :, :, q * 384 : q * 384 + 384].reshape(1024, 384)
        A0[0, xs, :, :, 0:384] = dot(n, PQK[...].reshape(1024, 384), TN).astype(BF).reshape(2, 4, 48, 384)
        A0[1, xs, :, :, 0:256] = dot(n, PV[...].reshape(1024, 256), TN).astype(BF).reshape(2, 4, 48, 256)
    A0[1, :, :, :, 256:384] = jnp.zeros((4, 4, 48, 128), BF)
    pair_start(0)
    gbuf[0, 0:4] = jnp.zeros((4, 768), F32)
    gbuf[0, 12:16] = jnp.zeros((4, 768), F32)
    mine = lax.broadcasted_iota(jnp.int32, (4, 1), 0) == z
    sq = colsum(PQK[...].reshape(1024, 384)[:, 0:256].astype(F32))
    sv = colsum(PV[...].reshape(1024, 256).astype(F32))
    gbuf[0, 12:16, 0:256] = jnp.where(mine, sq, 0.0)
    gbuf[0, 12:16, 256:512] = jnp.where(mine, sv, 0.0)
    turn(1, 1)

    second_moves = []
    for p in range(2):
        k1, k2 = kinds[p]
        wait(nb_moves[p])
        q = L.at("z", k2)
        NB(p, q)[...] = (NB(p, q)[...].astype(F32) + N1[p, 1].astype(F32)).astype(BF)
        second_moves.append(L.send(NB(p, q), N2.at[p], L.dev("z", k2)))
    pair_finish(0)
    turn(1, 2)
    for p in range(2):
        second_moves[p].wait_recv()
        rows_p = slice(p * 128, p * 128 + 128)
        nb = NB(p, z)[...].astype(F32) + N1[p, 0].astype(F32) + N2[p].astype(F32)
        xhat, r = norm_stats(tok[p].astype(F32))
        tgrad[p] = resid[rows_p] + norm_back(nb, xhat, r, g1)
        gbuf[0, 0:1] += colsum(nb * xhat)
        gbuf[0, 1:2] += colsum(nb)
    gsum.start(0)
    turn(0, 0)
    turn(1, 3)

    zb = [z0, z1, z2]
    W = [A0.at[c, x, y, :, pl.ds(384, 384)], A1.at[c, x, y], A2.at[c, x, y]]
    CUT = [(lanes(0, 128), lanes(128, 256)), (lanes(0, 768), lanes(768, 768)), (rows(0, 96), rows(96, 96))]
    zc, zc2 = {}, {}

    def z_start(i):
        zc[i] = [L.send(CUT[i][h](W[i]), CUT[i][h](zb[i].at[0]), L.dev("z", k)) for h, k in enumerate((1, 3))]

    def z_turn(i):
        zc2[i] = []
        for h, k in enumerate((3, 1)):
            q = zc[i][h]
            q.wait_recv()
            L.sent(q)
            v = CUT[i][h](W[i])
            v[...] = (v[...].astype(F32) + CUT[i][h](zb[i].at[0])[...].astype(F32)).astype(BF)
            zc2[i].append(L.send(v, CUT[i][h](zb[i].at[1]), L.dev("z", k)))

    fin, loc = [], []

    def hand(src, dst, nr):
        oth, ours = pl.multiple_of((1 - c) * nr, 8), pl.multiple_of(c * nr, 8)
        fin.append(L.send(src.at[..., pl.ds(oth, nr), :], dst.at[c], L.sib))
        loc.append(move(src.at[..., pl.ds(ours, nr), :], dst.at[c]))

    def z_finish(i, f, o, nr):
        for h in range(2):
            zc2[i][h].wait_recv()
            CUT[i][h](f)[...] = CUT[i][h](W[i])[...].astype(F32) + CUT[i][h](zb[i].at[1])[...].astype(F32)
        hand(f, o, nr)

    z_start(2)
    z_start(1)
    gsum.finish(0)
    gsum.start(1)
    turn(0, 1)
    z_turn(2)
    z_turn(1)
    gsum.finish(1)
    gsum.start(2)
    turn(0, 2)
    gsum.finish(2)
    gsum.start(3)
    turn(0, 3)
    z_start(0)
    zi[z] = A0[c, x, y, :, 0:384]
    zic = L.send(zi.at[z], zi.at[z], L.dev("z", 1))
    z_finish(2, f2f, o2, 96)
    z_finish(1, f1f, o1, 24)
    gsum.finish(3)
    gsum.start(4)
    z_turn(0)
    zic.wait_recv()
    zic2 = [L.send(zi.at[q], zi.at[q], L.dev("z", 3)) for q in (z, zf)]
    gsum.finish(4)
    gsum.start(5)
    z_finish(0, f0f, o0, 24)
    wait(zic2)
    fi[...] = zi[...].astype(F32)
    hand(fi, oi, 24)
    gsum.finish(5)
    gsum.start(6)
    wait(fin)
    for q in loc:
        q.wait()
    gsum.finish(6)
    osm[...] = gbuf[0]
    L.drain()


def layer(lengths, tokens, cot, w, wout, wexp, wshr, sm):
    V = pl.BlockSpec(memory_space=pltpu.VMEM)
    A = pl.BlockSpec(memory_space=pl.ANY)
    M = pl.BlockSpec(memory_space=pltpu.SMEM)
    S = jax.ShapeDtypeStruct
    b = lambda *s: pltpu.VMEM(s, BF)
    f = lambda *s: pltpu.VMEM(s, F32)
    scratch = [f(48, 384), f(48, 384), f(48, 1536), f(192, 384), f(6, 16, 768), f(8, 16, 768)]
    scratch += [b(2, 4, 4, *s) for s in SHAPES] * 2 + [b(4, 4, *s) for s in SHAPES]
    for s in SHAPES:
        scratch += [b(2, 4, *s), b(4, *s), b(2, *s), b(*s)]
    scratch += [b(4, 48, 384), b(2, 48, 384), b(2, 48, 1536), b(2, 192, 384)]
    scratch += [f(4, 48, 384), f(48, 384), f(48, 1536), f(192, 384)]
    scratch += [
        b(2, 4, 128, 768), b(2, 512, 384), b(2, 512, 256), b(6, 512, 512), f(512, 512),
        b(2, 4, 128, 192), b(4, 2, 128, 192), f(256, 768), f(256, 768), f(256, 1), b(256, 768), b(768, 256),
        b(256, 3072), b(256, 3072), b(256, 768), b(256, 768), b(2, 4, 128, 192), b(4, 2, 128, 192),
        b(2, 512, 384), b(2, 512, 256), b(2, 2, 128, 768), b(2, 128, 768),
    ]
    n = 300
    scratch += [pltpu.SemaphoreType.DMA((n,)), pltpu.SemaphoreType.DMA((n,)), pltpu.SemaphoreType.DMA((16,))]
    return pl.pallas_call(
        layer_kernel,
        out_shape=[
            S((2, 128, 768), BF), S((2, 128, 768), F32),
            S((2, 24, 384), F32), S((2, 4, 24, 384), F32), S((2, 24, 1536), F32), S((2, 96, 384), F32), S((16, 768), F32),
        ],
        in_specs=[M, A, V, V, A, A, A, A, V],
        out_specs=[V] * 7,
        scratch_shapes=scratch,
        compiler_params=pltpu.CompilerParams(collective_id=0, has_side_effects=True, vmem_limit_bytes=63 * 2**20),
        cost_estimate=pl.CostEstimate(flops=13 * 10**9, bytes_accessed=10**7, transcendentals=10**7),
    )(lengths, tokens, tokens, cot, w, wout, wexp, wshr, sm)


def spread(vectors, bias, me, z):
    base = lax.dynamic_update_slice(jnp.zeros((8, 768), F32), vectors.T, (0, me * 24))
    flat = lax.dynamic_update_slice(jnp.zeros((3072,), F32), bias, (me * 96,))
    part = lax.dynamic_slice(base, (2, z * 192), (2, 192))
    part = jnp.concatenate([part, jnp.zeros((2, 576), F32)], 1)
    return jnp.concatenate([base, flat.reshape(4, 768), part, jnp.zeros((2, 768), F32)], 0).astype(BF).astype(F32)


def body(tokens, cotangent, lengths, input_weight, output_weight, expand_weight, shrink_weight, vectors, expand_bias, *state):
    me = lax.axis_index("fsdp")
    z = lax.axis_index("ctx")
    w = lax.dynamic_slice_in_dim(input_weight.reshape(24, 3, 768), z * 192, 192, 2)
    w = jnp.concatenate([w.reshape(24, 576), jnp.zeros((24, 192), F32)], 1)
    small = spread(vectors, expand_bias, me, z)
    out, tokens_gradient, o0, oi, o1, o2, os_ = layer(
        lengths, tokens, cotangent, w, output_weight, expand_weight, shrink_weight, small
    )
    join = lambda a: jnp.moveaxis(a, 0, -2).reshape(a.shape[1:-1] + (-1,))
    full = join(oi)[:, :, :576].reshape(4, 24, 3, 192).transpose(1, 2, 0, 3).reshape(24, 2304)
    heads = os_[12:16, 0:512].reshape(4, 2, 256)[:, :, :192].transpose(1, 0, 2).reshape(2, 768)
    rows8 = jnp.concatenate([os_[0:2], heads, os_[4:8]], 0)
    vec = lax.dynamic_slice_in_dim(rows8, me * 24, 24, 1).T
    bia = lax.dynamic_slice_in_dim(os_[8:12].reshape(3072), me * 96, 96, 0)
    grads = (full, join(o0), join(o1), join(o2), vec, bia)
    weights = (input_weight, output_weight, expand_weight, shrink_weight, vectors, expand_bias)
    rates = (2.0 * D ** (-0.5), 4.0 * D ** (-0.5), 2.0 * D ** (-0.5), 2.0 * FF ** (-0.5), 1.0, 1.0)
    new = [adam_step(weights[i], grads[i], state[i], state[6 + i], rates[i]) for i in range(6)]
    return (out, tokens_gradient) + tuple(n[j] for j in range(3) for n in new)


def solution(mesh):
    in_specs = (
        P("fsdp", "ctx", None),
        P("fsdp", "ctx", None),
        P("fsdp", None),
        P("fsdp", None),
        P("fsdp", None),
        P("fsdp", None),
        P("fsdp", None),
        P("fsdp", None),
        P("fsdp"),
        P("fsdp", None),
        P("fsdp", None),
        P("fsdp", None),
        P("fsdp", None),
        P("fsdp", None),
        P("fsdp"),
        P("fsdp", None),
        P("fsdp", None),
        P("fsdp", None),
        P("fsdp", None),
        P("fsdp", None),
        P("fsdp"),
    )
    out_specs = (
        P("fsdp", "ctx", None),
        P("fsdp", "ctx", None),
        P("fsdp", None),
        P("fsdp", None),
        P("fsdp", None),
        P("fsdp", None),
        P("fsdp", None),
        P("fsdp"),
        P("fsdp", None),
        P("fsdp", None),
        P("fsdp", None),
        P("fsdp", None),
        P("fsdp", None),
        P("fsdp"),
        P("fsdp", None),
        P("fsdp", None),
        P("fsdp", None),
        P("fsdp", None),
        P("fsdp", None),
        P("fsdp"),
    )
    return jax.shard_map(body, mesh=mesh, in_specs=in_specs, out_specs=out_specs, check_vma=False)
```

profile of v0, /device:TPU:0, one launch (start us, length us, event | category | flops | bytes accessed | tf_op | source)
XLA Modules:
  0.0 155.2 jit_solution(65320114669136486)
XLA Ops:
  0.7 1.1 reshape.77
  1.7 0.1 constant_dynamic-slice_fusion
  1.8 0.1 reshape.78
  2.0 0.6 concatenate.13.win
  2.6 0.7 copy-done.18
  3.4 0.1 dynamic-slice_convert_fusion
  3.5 0.7 copy-done.21
  4.1 0.2 dynamic_update_slice.7
  4.4 0.7 fusion.8.sm
  5.1 138.3 %shard_map.356 = (bf16[2,128,768]{2,1,0:T(8,128)(2,1)}, f32[2,128,768]{2,1,0:T(8,128)}, f32[2,24,384]{2,1,0:T(8,128)}, f32[2,4,24,384]{3,2,1,0:T(8,128)}, f32[2,...) custom-call(s32[2,4]{1,0:T(2,128)} %lengths.1, bf16[2,128,768]{2,1,0:T(8,128)(2,1)} %tok.1, ...), custom_call_target="tpu_custom_call" | custom-call | flops 12999999488 | bytes 10000000 | tf_op jit(solution)/shard_map/pallas_call | solution.py:728
  143.4 1.0 copy.53
  144.4 0.2 reshape.81
  144.6 0.2 copy.48
  144.8 0.2 reshape.82
  145.0 0.5 copy-done.12
  145.5 0.2 copy-done
  145.8 0.1 copy-done.11
  145.9 0.9 multiply_subtract_fusion.2
  147.0 0.7 multiply_subtract_fusion.3
  147.7 0.1 copy-done.4
  147.9 0.9 copy-done.5
  148.8 0.1 copy-done.6
  148.9 1.0 multiply_subtract_fusion.1
  150.0 0.2 copy-done.10
  150.1 0.8 copy-done.8
  150.9 0.1 copy-done.9
  151.1 1.0 multiply_subtract_fusion
  152.2 0.1 reshape.87
  152.3 0.7 add_subtract_fusion
  153.0 0.6 add_subtract_fusion.1
  153.6 0.7 copy.61
  154.3 0.9 copy.62
  (52 shorter events, 0.5 us)
Async XLA Ops:
  2.6 0.7 copy-start.18
  3.5 0.7 copy-start.21
  144.6 0.9 copy-start.12
  144.8 1.0 copy-start
  144.8 1.1 copy-start.11
  145.9 0.9 copy-start.13
  145.9 1.0 copy-start.14
  145.9 1.0 copy-start.15
  145.9 1.1 copy-start.16
  146.8 1.1 copy-start.7
  146.8 1.0 copy-start.4
  147.9 1.0 copy-start.5
  147.9 1.1 copy-start.6
  148.9 1.0 copy-start.3
  148.9 1.2 copy-start.10
  150.0 1.0 copy-start.8
  150.0 1.1 copy-start.9
  151.0 1.1 copy-start.17
  151.0 1.2 copy-start.19
  151.0 1.2 copy-start.20
  151.0 1.9 %copy-start.22 = (f32[96]{0:T(128)S(1)}, f32[96]{0:T(128)}, u32[]{:S(2)}) copy-start(f32[96]{0:T(128)} %param.35) | copy-start | bytes 1156
  151.0 1.9 %copy-start.23 = (f32[96]{0:T(128)S(1)}, f32[96]{0:T(128)}, u32[]{:S(2)}) copy-start(f32[96]{0:T(128)} %param.41) | copy-start | bytes 1156
  151.1 2.5 %copy-start.2 = (bf16[2,128,768]{2,1,0:T(8,128)(2,1)S(1)}, bf16[2,128,768]{2,1,0:T(8,128)(2,1)}, u32[]{:S(2)}) copy-start(bf16[2,128,768]{2,1,0:T(8,128)(2,1)} %get-tuple-element.74) | copy-start | bytes 1179652
  152.1 2.2 %copy-start.1 = (f32[2,128,768]{2,1,0:T(8,128)S(1)}, f32[2,128,768]{2,1,0:T(8,128)}, u32[]{:S(2)}) copy-start(f32[2,128,768]{2,1,0:T(8,128)} %get-tuple-element.75) | copy-start | bytes 2359300
where the time goes:
time: 156 us; the launch traced here: 155 us
  Pallas kernels  138 us (88%)
  local copies, waits for them, and re-layouts  10.3 us (7%)
  other arithmetic  5.74 us (4%)
    pallas_call x1, Pallas kernels, layer(): pl.pallas_call(layer_kernel, out_shape=[S((2, 128, 768), BF), S((2, 128,...  138 us
    unnamed x50, local copies, waits for them, and re-layouts  6.23 us
    sub x6, other arithmetic, adam_step(): weight - rate * (corrected / spread + decay_rate * weight)  5.04 us

commit v1 on v0

--- a/solution.py
+++ b/solution.py
@@ -34,6 +34,15 @@
         x = self.at("x", kind) if axis == "x" else self.x
         y = self.at("y", kind) if axis == "y" else self.y
         return {"fsdp": (x * 4 + y) * 2 + self.core}
+
+    def peers(self, axis):
+        v = {"x": self.x, "y": self.y, "z": self.z}[axis]
+        others = [flip1(v), 3 - v, (v + 2) % 4]
+        if axis == "z":
+            return [{"ctx": o} for o in others]
+        if axis == "x":
+            return [{"fsdp": (o * 4 + self.y) * 2 + self.core} for o in others]
+        return [{"fsdp": (self.x * 4 + o) * 2 + self.core} for o in others]
 
     def send(self, src, dst, device):
         i = self.used
@@ -173,7 +182,7 @@
 
 
 PIECES = (
-    tuple((f, lanes(f * 128, 128)) for f in range(3)) + ((3, lanes(384, 384)),),
+    tuple((f, lanes(f * 128, 128)) for f in range(3)) + tuple((3 - f, lanes(384 + f * 128, 128)) for f in range(3)),
     tuple((f, lanes(f * 384, 384)) for f in range(4)),
     tuple((f, rows(f * 48, 48)) for f in range(4)),
 )
@@ -229,9 +238,9 @@
 
 
 def layer_kernel(
-    lengths, tok_hbm, tok, cot, win, wout, wexp, wshr, sm,
+    lengths, tok, cot, win_all, wout, wexp, wshr, vecs, bias_in,
     out, tgrad, o0, oi, o1, o2, osm,
-    f0a, f0b, f1, f2, sbuf, gbuf,
+    win, f0a, f0b, f1, f2, sbuf, gbuf,
     G0, G1, G2, A0, A1, A2, S0, S1, S2,
     R00, R01, R02, R03, R10, R11, R12, R13, R20, R21, R22, R23,
     zi, z0, z1, z2, fi, f0f, f1f, f2f,
@@ -243,7 +252,6 @@
     me = {"x": x, "y": y}
     zf, zt, zo = L.at("z", 1), L.at("z", 3), (z + 2) % 4
     zpeers = (zf, zt, zo)
-    L.barrier([L.sib] + [L.dev(a, k) for a in "xyz" for k in (1, 3)] + [{"ctx": zo}])
     G, A, S = [G0, G1, G2], [A0, A1, A2], [S0, S1, S2]
 
     def wait(copies):
@@ -258,23 +266,48 @@
         cp.start()
         return cp
 
-    stages = [L.sib] + [L.dev(a, k) for a, k in (("y", 1), ("y", 3), ("x", 1), ("x", 3), ("z", 1), ("z", 3))]
-
     class Sum:
         def __init__(self, buf):
             self.buf = buf
 
-        def start(self, i):
-            self.copy = L.send(self.buf.at[0], self.buf.at[i + 1], stages[i])
-
-        def finish(self, i):
-            self.copy.wait_recv()
-            L.sent(self.copy)
-            self.buf[0] = self.buf[0] + self.buf[i + 1]
+        def start(self, axis):
+            base = 1 + 4 * "cyxz".index(axis)
+            v, to = {"c": (c, [L.sib]), "x": (x, L.peers("x")), "y": (y, L.peers("y")), "z": (z, L.peers("z"))}[axis]
+            self.buf[base + v] = self.buf[0]
+            self.slots = [base + i for i in range(len(to) + 1)]
+            self.copies = [L.send(self.buf.at[base + v], self.buf.at[base + v], d) for d in to]
+
+        def finish(self):
+            wait(self.copies)
+            total = self.buf[self.slots[0]]
+            for i in self.slots[1:]:
+                total = total + self.buf[i]
+            self.buf[0] = total
 
     small = Sum(sbuf)
-    sbuf[0] = sm[...]
-    small.start(0)
+    me_all = lax.axis_index("fsdp")
+    tiled = vecs[...]
+    for _ in range(5):
+        tiled = jnp.concatenate([tiled, tiled], 1)
+    lane = lax.broadcasted_iota(jnp.int32, (1, 768), 1)
+    first = me_all * 24
+    sbuf[0] = jnp.zeros((16, 768), F32)
+    sbuf[0, 0:8] = jnp.where((lane >= first) & (lane < first + 24), tiled, 0.0)
+    near = (lane + z * 192 >= first) & (lane + z * 192 < first + 24) & (lane < 192)
+    sbuf[0, 12:14] = jnp.where(near, tiled[2:4], 0.0)
+    tiled = jnp.broadcast_to(bias_in[...], (4, 96))
+    for _ in range(3):
+        tiled = jnp.concatenate([tiled, tiled], 1)
+    first = (me_all % 8) * 96
+    here = (lax.broadcasted_iota(jnp.int32, (4, 1), 0) == me_all // 8) & (lane >= first) & (lane < first + 96)
+    sbuf[0, 8:12] = jnp.where(here, tiled, 0.0)
+    sbuf[0] = sbuf[0].astype(BF).astype(F32)
+    for j in range(3):
+        cut = [win_all[:, j * 768 + q * 192 : j * 768 + q * 192 + 192] for q in range(4)]
+        win[:, j * 192 : j * 192 + 192] = jnp.where(z == 0, cut[0], jnp.where(z == 1, cut[1], jnp.where(z == 2, cut[2], cut[3])))
+    win[:, 576:768] = jnp.zeros((24, 192), F32)
+    L.barrier([L.sib] + L.peers("x") + L.peers("y") + L.peers("z"))
+    small.start("c")
 
     def halves(src, n, dst, nr):
         other, mine = pl.multiple_of((1 - c) * n, 128), pl.multiple_of(c * n, 128)
@@ -282,12 +315,12 @@
         return L.send(src.at[:, pl.ds(other, n)], dst.at[r], L.sib), move(src.at[:, pl.ds(mine, n)], dst.at[r])
 
     pairs = [halves(win, 384, f0a, 24), halves(wout, 384, f0b, 24)]
-    xl = move(tok_hbm, X.at[:, z])
+    xl = move(tok, X.at[:, z])
     tz = []
     for p in range(2):
         for h, k in enumerate((1, 3)):
             r = pl.ds(h * 64, 64)
-            tz.append(L.send(tok_hbm.at[p, r], X.at[p, z, r], L.dev("z", k)))
+            tz.append(L.send(tok.at[p, r], X.at[p, z, r], L.dev("z", k)))
     pairs += [halves(wexp, 1536, f1, 24), halves(wshr, 384, f2, 96)]
 
     views = []
@@ -319,8 +352,8 @@
     G0[c, x, y, :, 0:384] = f0a[...].astype(BF)
     G0[c, x, y, :, 384:768] = f0b[...].astype(BF)
     start(0, 0)
-    small.finish(0)
-    small.start(1)
+    small.finish()
+    small.start("y")
     for g, f in ((1, f1), (2, f2)):
         cp, lc = pairs[g + 1]
         cp.wait_recv()
@@ -328,8 +361,8 @@
         G[g][c, x, y] = f[...].astype(BF)
         start(g, 0)
     advance(0, 1)
-    small.finish(1)
-    small.start(2)
+    small.finish()
+    small.start("x")
     xl.wait()
     tz2 = []
     for p in range(2):
@@ -339,14 +372,10 @@
             q = L.at("z", k1)
             tz2.append([L.send(X.at[p, b, r], X.at[p, b, r], L.dev("z", k2)) for b in (z, q)])
     advance(0, 2)
-    small.finish(2)
-    small.start(3)
     advance(1, 1)
     advance(2, 1)
     advance(0, 3)
     sib = {0: to_sibling(0, False)}
-    small.finish(3)
-    small.start(4)
 
     seqs = lengths.shape[1]
 
@@ -371,7 +400,7 @@
             total = total + lengths[p, i]
         return (pos < total).astype(F32)
 
-    small.finish(4)
+    small.finish()
     g1, b1 = sbuf[0, 0:1], sbuf[0, 1:2]
 
     def ready(p):
@@ -437,8 +466,6 @@
     own.append(move(CS.at[1, z], CT.at[z, 1]))
     wait(flight[1])
     sib[1] += to_sibling(1, True)
-    wait(flight[2])
-    sib[2] += to_sibling(2, True)
     for q in own:
         q.wait()
     wait(ctx_moves)
@@ -466,8 +493,6 @@
         cdf = 0.5 * (1.0 + lax.erf(e * (2.0 ** -0.5)))
         hidden[:, t * 768 : t * 768 + 768] = (e * cdf).astype(BF)
         slope[:, t * 768 : t * 768 + 768] = (cdf + e * (jnp.exp(-0.5 * e * e) * 0.3989422804014327)).astype(BF)
-    wait(sib[2])
-
     for t in range(4):
         for h in range(2):
             d = dot(hidden[:, t * 768 : t * 768 + 768], up[:, h * 384 : h * 384 + 384], TN)
@@ -477,18 +502,28 @@
         return [(f, (lambda sub: lambda xs, ys: sub(A[i].at[c, xs, ys]))(sub), sub) for f, sub in PIECES[i]]
 
     bufs = [[R00, R01, R02, R03], [R10, R11, R12, R13], [R20, R21, R22, R23]]
-    sc = [Scatter(L, pieces_of(i), bufs[i]) for i in range(3)]
+    sc = {1: Scatter(L, pieces_of(1), bufs[1]), 2: Scatter(L, pieces_of(2), bufs[2])}
+    sc["in"] = Scatter(L, pieces_of(0)[:3], bufs[0])
+    sc["out"] = Scatter(L, pieces_of(0)[3:], bufs[0])
     pair = {}
+    split = {"in": lanes(0, 384), "out": lanes(384, 384)}
 
     def pair_start(i):
-        pair[i] = L.send(A[i].at[1 - c], S[i], L.sib)
+        if i in split:
+            pair[i] = L.send(split[i](A0.at[1 - c]), split[i](S0), L.sib)
+        else:
+            pair[i] = L.send(A[i].at[1 - c], S[i], L.sib)
 
     def pair_finish(i):
         pair[i].wait_recv()
 
         @pl.loop(0, 4)
         def _(k):
-            A[i][c, k] = (A[i][c, k].astype(F32) + S[i][k].astype(F32)).astype(BF)
+            if i in split:
+                a, b = split[i](A0.at[c, k]), split[i](S0.at[k])
+            else:
+                a, b = A[i].at[c, k], S[i].at[k]
+            a[...] = (a[...].astype(F32) + b[...].astype(F32)).astype(BF)
 
         sc[i].start(0)
 
@@ -498,6 +533,11 @@
             sc[i].start(s + 1)
 
     pair_start(2)
+
+    wait(flight[2])
+    sib[2] += to_sibling(2, True)
+    pair_finish(2)
+    wait(sib[2])
 
     for h in range(2):
         w = after[:, h * 384 : h * 384 + 384] + bd[:, h * 384 : h * 384 + 384]
@@ -505,7 +545,6 @@
             w = w + dot(hidden[:, t * 768 : t * 768 + 768], G2[h, t].reshape(768, 384), NN)
         for p in range(2):
             out[p, :, h * 384 : h * 384 + 384] = (w[p * 128 : p * 128 + 128] * live[p]).astype(BF)
-    pair_finish(2)
 
     resid = after
     gsum = Sum(gbuf)
@@ -546,8 +585,10 @@
         d = dot(CT[q].reshape(256, 192), ab[...], TN).astype(BF)
         for h in range(2):
             A0[h, q, :, :, 384:768] = d[:, h * 384 : h * 384 + 384].reshape(4, 48, 384)
+    pair_start("out")
     pair_finish(1)
     turn(2, 1)
+    pair_finish("out")
 
     def attend_back(p):
         co = CB[:, p].reshape(512, 192)
@@ -595,15 +636,15 @@
         wait(back_moves[p])
         attend_back(p)
         inner_back(p)
-        turn(2, 2 + p)
         if p == 0:
+            turn(2, 2)
             turn(1, 0)
     for q in range(2):
         xs, n = slice(2 * q, 2 * q + 2), X[:, :, :, q * 384 : q * 384 + 384].reshape(1024, 384)
         A0[0, xs, :, :, 0:384] = dot(n, PQK[...].reshape(1024, 384), TN).astype(BF).reshape(2, 4, 48, 384)
         A0[1, xs, :, :, 0:256] = dot(n, PV[...].reshape(1024, 256), TN).astype(BF).reshape(2, 4, 48, 256)
     A0[1, :, :, :, 256:384] = jnp.zeros((4, 4, 48, 128), BF)
-    pair_start(0)
+    pair_start("in")
     gbuf[0, 0:4] = jnp.zeros((4, 768), F32)
     gbuf[0, 12:16] = jnp.zeros((4, 768), F32)
     mine = lax.broadcasted_iota(jnp.int32, (4, 1), 0) == z
@@ -611,29 +652,6 @@
     sv = colsum(PV[...].reshape(1024, 256).astype(F32))
     gbuf[0, 12:16, 0:256] = jnp.where(mine, sq, 0.0)
     gbuf[0, 12:16, 256:512] = jnp.where(mine, sv, 0.0)
-    turn(1, 1)
-
-    second_moves = []
-    for p in range(2):
-        k1, k2 = kinds[p]
-        wait(nb_moves[p])
-        q = L.at("z", k2)
-        NB(p, q)[...] = (NB(p, q)[...].astype(F32) + N1[p, 1].astype(F32)).astype(BF)
-        second_moves.append(L.send(NB(p, q), N2.at[p], L.dev("z", k2)))
-    pair_finish(0)
-    turn(1, 2)
-    for p in range(2):
-        second_moves[p].wait_recv()
-        rows_p = slice(p * 128, p * 128 + 128)
-        nb = NB(p, z)[...].astype(F32) + N1[p, 0].astype(F32) + N2[p].astype(F32)
-        xhat, r = norm_stats(tok[p].astype(F32))
-        tgrad[p] = resid[rows_p] + norm_back(nb, xhat, r, g1)
-        gbuf[0, 0:1] += colsum(nb * xhat)
-        gbuf[0, 1:2] += colsum(nb)
-    gsum.start(0)
-    turn(0, 0)
-    turn(1, 3)
-
     zb = [z0, z1, z2]
     W = [A0.at[c, x, y, :, pl.ds(384, 384)], A1.at[c, x, y], A2.at[c, x, y]]
     CUT = [(lanes(0, 128), lanes(128, 256)), (lanes(0, 768), lanes(768, 768)), (rows(0, 96), rows(96, 96))]
@@ -665,53 +683,72 @@
             CUT[i][h](f)[...] = CUT[i][h](W[i])[...].astype(F32) + CUT[i][h](zb[i].at[1])[...].astype(F32)
         hand(f, o, nr)
 
+    turn(2, 3)
     z_start(2)
+    turn("out", 0)
+    turn(1, 1)
+    pair_finish("in")
+    turn("out", 1)
+
+    second_moves = []
+    for p in range(2):
+        k1, k2 = kinds[p]
+        wait(nb_moves[p])
+        q = L.at("z", k2)
+        NB(p, q)[...] = (NB(p, q)[...].astype(F32) + N1[p, 1].astype(F32)).astype(BF)
+        second_moves.append(L.send(NB(p, q), N2.at[p], L.dev("z", k2)))
+    turn(1, 2)
+    turn("out", 2)
+    turn("in", 0)
+    z_turn(2)
+    turn(1, 3)
     z_start(1)
-    gsum.finish(0)
-    gsum.start(1)
-    turn(0, 1)
-    z_turn(2)
+    turn("out", 3)
+    z_start(0)
+    turn("in", 1)
+    z_finish(2, f2f, o2, 96)
+    turn("in", 2)
     z_turn(1)
-    gsum.finish(1)
-    gsum.start(2)
-    turn(0, 2)
-    gsum.finish(2)
-    gsum.start(3)
-    turn(0, 3)
-    z_start(0)
+    z_turn(0)
+    for p in range(2):
+        second_moves[p].wait_recv()
+        rows_p = slice(p * 128, p * 128 + 128)
+        nb = NB(p, z)[...].astype(F32) + N1[p, 0].astype(F32) + N2[p].astype(F32)
+        xhat, r = norm_stats(tok[p].astype(F32))
+        tgrad[p] = resid[rows_p] + norm_back(nb, xhat, r, g1)
+        gbuf[0, 0:1] += colsum(nb * xhat)
+        gbuf[0, 1:2] += colsum(nb)
+    gsum.start("c")
+    turn("in", 3)
     zi[z] = A0[c, x, y, :, 0:384]
-    zic = L.send(zi.at[z], zi.at[z], L.dev("z", 1))
-    z_finish(2, f2f, o2, 96)
+    zic = [L.send(zi.at[z], zi.at[z], d) for d in L.peers("z")]
+    gsum.finish()
+    gsum.start("z")
     z_finish(1, f1f, o1, 24)
-    gsum.finish(3)
-    gsum.start(4)
-    z_turn(0)
-    zic.wait_recv()
-    zic2 = [L.send(zi.at[q], zi.at[q], L.dev("z", 3)) for q in (z, zf)]
-    gsum.finish(4)
-    gsum.start(5)
     z_finish(0, f0f, o0, 24)
-    wait(zic2)
+    wait(zic)
     fi[...] = zi[...].astype(F32)
     hand(fi, oi, 24)
-    gsum.finish(5)
-    gsum.start(6)
+    gsum.finish()
+    gsum.start("y")
+    gsum.finish()
+    gsum.start("x")
     wait(fin)
     for q in loc:
         q.wait()
-    gsum.finish(6)
+    gsum.finish()
     osm[...] = gbuf[0]
     L.drain()
 
 
-def layer(lengths, tokens, cot, w, wout, wexp, wshr, sm):
+def layer(lengths, tokens, cot, w, wout, wexp, wshr, vecs, bias_in):
     V = pl.BlockSpec(memory_space=pltpu.VMEM)
-    A = pl.BlockSpec(memory_space=pl.ANY)
+    A = pl.BlockSpec(memory_space=pltpu.HBM)
     M = pl.BlockSpec(memory_space=pltpu.SMEM)
     S = jax.ShapeDtypeStruct
     b = lambda *s: pltpu.VMEM(s, BF)
     f = lambda *s: pltpu.VMEM(s, F32)
-    scratch = [f(48, 384), f(48, 384), f(48, 1536), f(192, 384), f(6, 16, 768), f(8, 16, 768)]
+    scratch = [f(24, 768), f(48, 384), f(48, 384), f(48, 1536), f(192, 384), f(13, 16, 768), f(17, 16, 768)]
     scratch += [b(2, 4, 4, *s) for s in SHAPES] * 2 + [b(4, 4, *s) for s in SHAPES]
     for s in SHAPES:
         scratch += [b(2, 4, *s), b(4, *s), b(2, *s), b(*s)]
@@ -731,42 +768,103 @@
             S((2, 128, 768), BF), S((2, 128, 768), F32),
             S((2, 24, 384), F32), S((2, 4, 24, 384), F32), S((2, 24, 1536), F32), S((2, 96, 384), F32), S((16, 768), F32),
         ],
-        in_specs=[M, A, V, V, A, A, A, A, V],
+        in_specs=[M, V, V, V, A, A, A, V, V],
         out_specs=[V] * 7,
         scratch_shapes=scratch,
         compiler_params=pltpu.CompilerParams(collective_id=0, has_side_effects=True, vmem_limit_bytes=63 * 2**20),
         cost_estimate=pl.CostEstimate(flops=13 * 10**9, bytes_accessed=10**7, transcendentals=10**7),
-    )(lengths, tokens, tokens, cot, w, wout, wexp, wshr, sm)
-
-
-def spread(vectors, bias, me, z):
-    base = lax.dynamic_update_slice(jnp.zeros((8, 768), F32), vectors.T, (0, me * 24))
-    flat = lax.dynamic_update_slice(jnp.zeros((3072,), F32), bias, (me * 96,))
-    part = lax.dynamic_slice(base, (2, z * 192), (2, 192))
-    part = jnp.concatenate([part, jnp.zeros((2, 576), F32)], 1)
-    return jnp.concatenate([base, flat.reshape(4, 768), part, jnp.zeros((2, 768), F32)], 0).astype(BF).astype(F32)
+    )(lengths, tokens, cot, w, wout, wexp, wshr, vecs, bias_in)
+
+
+def adam_kernel(o0, oi, o1, o2, osm, out, tgrad, *refs):
+    me = lax.axis_index("fsdp")
+    ins, outs, bufs, in_sem, out_sem = refs[0:18], refs[20:38], refs[38:56], refs[58], refs[59]
+    loads = [pltpu.make_async_copy(ins[k], bufs[k], in_sem.at[k]) for k in range(18)]
+    fetch = [pltpu.make_async_copy(a, refs[56 + k], in_sem.at[18 + k]) for k, a in enumerate((out, tgrad))]
+    passed = [pltpu.make_async_copy(refs[56 + k], refs[18 + k], out_sem.at[18 + k]) for k in range(2)]
+    order = (3, 2, 0, 1, 4, 5)
+    for i in order:
+        for j in range(3):
+            loads[6 * j + i].start()
+    for q in fetch:
+        q.start()
+    w, m, s = bufs[0:6], bufs[6:12], bufs[12:18]
+    stores = []
+
+    def arrived(i):
+        for j in range(3):
+            loads[6 * j + i].wait()
+
+    def leave(i):
+        for j in range(3):
+            k = 6 * j + i
+            stores.append(pltpu.make_async_copy(bufs[k], outs[k], out_sem.at[k]))
+            stores[-1].start()
+
+    rates = (2.0 * D ** (-0.5), 4.0 * D ** (-0.5), 2.0 * D ** (-0.5), 2.0 * FF ** (-0.5), 1.0, 1.0)
+
+    def step(i, cols, gradient):
+        new = adam_step(w[i][:, cols], gradient, m[i][:, cols], s[i][:, cols], rates[i])
+        for j in range(3):
+            bufs[6 * j + i][:, cols] = new[j]
+
+    for i, o, n in ((3, o2, 384), (2, o1, 1536)):
+        arrived(i)
+        for h in range(2):
+            step(i, slice(h * n, h * n + n), o[h])
+        leave(i)
+    arrived(0)
+    for j, (h, lane) in enumerate(((0, 0), (0, 192), (1, 0))):
+        g = jnp.concatenate([oi[h, q, :, lane : lane + 192] for q in range(4)], 1)
+        step(0, slice(j * 768, j * 768 + 768), g)
+    leave(0)
+    for a, b in zip(fetch, passed):
+        a.wait()
+        b.start()
+    arrived(1)
+    for h in range(2):
+        step(1, slice(h * 384, h * 384 + 384), o0[h])
+    leave(1)
+    heads = [jnp.concatenate([osm[12 + q : 13 + q, n : n + 192] for q in range(4)], 1) for n in (0, 256)]
+    rows8 = jnp.concatenate([osm[0:2]] + heads + [osm[4:8]], 0)
+    rows8 = pltpu.roll(rows8, ((32 - me) % 32) * 24, 1)[:, 0:128]
+    arrived(4)
+    step(4, slice(0, 24), rows8[:, 0:24])
+    leave(4)
+    pick = lax.broadcasted_iota(jnp.int32, (4, 1), 0) == me // 8
+    row = jnp.sum(jnp.where(pick, osm[8:12], 0.0), 0, keepdims=True)
+    row = pltpu.roll(jnp.broadcast_to(row, (8, 768)), ((8 - me % 8) % 8) * 96, 1)
+    arrived(5)
+    step(5, slice(0, 96), row[0:1, 0:96])
+    leave(5)
+    for q in passed + stores:
+        q.wait()
+
+
+def adam(grads, out, tgrad, weights, moments, squares):
+    args = weights + moments + squares
+    V = pl.BlockSpec(memory_space=pltpu.VMEM)
+    B = pl.BlockSpec(memory_space=pltpu.HBM)
+    n = len(args)
+    return pl.pallas_call(
+        adam_kernel,
+        out_shape=[jax.ShapeDtypeStruct(a.shape, a.dtype) for a in [out, tgrad] + args],
+        in_specs=[V] * 5 + [B] * (2 + n),
+        out_specs=[B] * (2 + n),
+        scratch_shapes=[pltpu.VMEM(a.shape, a.dtype) for a in args + [out, tgrad]] + [pltpu.SemaphoreType.DMA((20,))] * 2,
+        compiler_params=pltpu.CompilerParams(vmem_limit_bytes=63 * 2**20),
+    )(*grads, out, tgrad, *args)
 
 
 def body(tokens, cotangent, lengths, input_weight, output_weight, expand_weight, shrink_weight, vectors, expand_bias, *state):
-    me = lax.axis_index("fsdp")
-    z = lax.axis_index("ctx")
-    w = lax.dynamic_slice_in_dim(input_weight.reshape(24, 3, 768), z * 192, 192, 2)
-    w = jnp.concatenate([w.reshape(24, 576), jnp.zeros((24, 192), F32)], 1)
-    small = spread(vectors, expand_bias, me, z)
     out, tokens_gradient, o0, oi, o1, o2, os_ = layer(
-        lengths, tokens, cotangent, w, output_weight, expand_weight, shrink_weight, small
+        lengths, tokens, cotangent, input_weight, output_weight, expand_weight, shrink_weight, vectors.T, expand_bias.reshape(1, 96)
     )
-    join = lambda a: jnp.moveaxis(a, 0, -2).reshape(a.shape[1:-1] + (-1,))
-    full = join(oi)[:, :, :576].reshape(4, 24, 3, 192).transpose(1, 2, 0, 3).reshape(24, 2304)
-    heads = os_[12:16, 0:512].reshape(4, 2, 256)[:, :, :192].transpose(1, 0, 2).reshape(2, 768)
-    rows8 = jnp.concatenate([os_[0:2], heads, os_[4:8]], 0)
-    vec = lax.dynamic_slice_in_dim(rows8, me * 24, 24, 1).T
-    bia = lax.dynamic_slice_in_dim(os_[8:12].reshape(3072), me * 96, 96, 0)
-    grads = (full, join(o0), join(o1), join(o2), vec, bia)
+    flat = lambda t: list(t[:4]) + [t[4].T, t[5].reshape(1, 96)]
     weights = (input_weight, output_weight, expand_weight, shrink_weight, vectors, expand_bias)
-    rates = (2.0 * D ** (-0.5), 4.0 * D ** (-0.5), 2.0 * D ** (-0.5), 2.0 * FF ** (-0.5), 1.0, 1.0)
-    new = [adam_step(weights[i], grads[i], state[i], state[6 + i], rates[i]) for i in range(6)]
-    return (out, tokens_gradient) + tuple(n[j] for j in range(3) for n in new)
+    new = adam([o0, oi, o1, o2, os_], out, tokens_gradient, flat(weights), flat(state[:6]), flat(state[6:]))
+    fix = {4: lambda a: a.T, 5: lambda a: a.reshape(96)}
+    return tuple(new[:2]) + tuple(fix.get(i % 6, lambda a: a)(a) for i, a in enumerate(new[2:]))
 
 
 def solution(mesh):

time: 156 us -> 133 us (0.85)
  local copies, waits for them, and re-layouts: 10.3 us -> 0 us
  Pallas kernels: 138 us -> 132 us
  other arithmetic: 5.74 us -> 0 us
    pallas_call x1, Pallas kernels: 138 us -> 127 us  [layer(): pl.pallas_call(layer_kernel, out_shape=[S((2, 128, 768), BF), S((2, 128,...]
    unnamed x50 -> x0, local copies, waits for them, and re-layouts: 6.23 us -> none
    sub x6 -> x0, other arithmetic: 5.04 us -> none  [adam_step(): weight - rate * (corrected / spread + decay_rate * weight)]
    pallas_call x0 -> x1, Pallas kernels: none -> 4.9 us  [adam(): pl.pallas_call(adam_kernel, out_shape=[jax.ShapeDtypeStruct(a.shape, a.dt...]
    reshape x11 -> x0, local copies, waits for them, and re-layouts: 2.66 us -> none  [the longest x1 1.05 us: body(): input_weight.reshape(24, 3, 768)]
where the time goes in v1:
time: 133 us
  Pallas kernels  132 us (99%)
    pallas_call x1, Pallas kernels, layer(): pl.pallas_call(layer_kernel, out_shape=[S((2, 128, 768), BF), S((2, 128,...  127 us
    pallas_call x1, Pallas kernels, adam(): pl.pallas_call(adam_kernel, out_shape=[jax.ShapeDtypeStruct(a.shape, a.dt...  4.9 us

profile of v1, /device:TPU:0, one launch (start us, length us, event | category | flops | bytes accessed | tf_op | source)
XLA Modules:
  0.0 133.3 jit_solution(5953291274469252766)
XLA Ops:
  0.7 127.5 %shard_map.356 = (bf16[2,128,768]{2,1,0:T(8,128)(2,1)}, f32[2,128,768]{2,1,0:T(8,128)}, f32[2,24,384]{2,1,0:T(8,128)}, f32[2,4,24,384]{3,2,1,0:T(8,128)}, f32[2,...) custom-call(s32[2,4]{1,0:T(2,128)} %lengths.1, bf16[2,128,768]{2,1,0:T(8,128)(2,1)} %tok.1, ...), custom_call_target="tpu_custom_call" | custom-call | flops 12999999488 | bytes 10000000 | tf_op jit(solution)/shard_map/pallas_call | solution.py:765
  128.2 4.9 %shard_map.357 = (bf16[2,128,768]{2,1,0:T(8,128)(2,1)}, f32[2,128,768]{2,1,0:T(8,128)}, f32[24,2304]{1,0:T(8,128)}, f32[24,768]{1,0:T(8,128)}, f32[24,3072]{1,0:...) custom-call(f32[2,24,384]{2,1,0:T(8,128)} %get-tuple-element.47.o0, ...), custom_call_target="tpu_custom_call" | custom-call | tf_op jit(solution)/shard_map/pallas_call | solution.py:849

commit v2 on v1

--- a/solution.py
+++ b/solution.py
@@ -441,20 +441,20 @@
         res = [L.send(src.at[p, q], dst.at[z, p], {"ctx": q}) for q in zpeers]
         return res
 
+    fill_mask(0)
+    advance(1, 2)
+    advance(2, 2)
+    wait(flight[0])
+    sib[0] += to_sibling(0, True)
     ready(0)
     project(0)
-    wait(flight[0])
-    sib[0] += to_sibling(0, True)
-    advance(1, 2)
-    advance(2, 2)
-    fill_mask(0)
     wait(sib[0])
     qkv(0)
+    advance(1, 3)
+    sib[1] = to_sibling(1, False)
     attend(0)
     ctx_moves = to_heads_owner(0, CS, CT)
     own = [move(CS.at[0, z], CT.at[z, 0])]
-    advance(1, 3)
-    sib[1] = to_sibling(1, False)
     advance(2, 3)
     sib[2] = to_sibling(2, False)
     ready(1)

time: 133 us -> 131 us (0.985)
  Pallas kernels: 132 us -> 130 us
    pallas_call x1, Pallas kernels: 127 us -> 125 us  [layer(): pl.pallas_call(layer_kernel, out_shape=[S((2, 128, 768), BF), S((2, 128,...]
where the time goes in v2:
time: 131 us
  Pallas kernels  130 us (99%)
    pallas_call x1, Pallas kernels, layer(): pl.pallas_call(layer_kernel, out_shape=[S((2, 128, 768), BF), S((2, 128,...  125 us
    pallas_call x1, Pallas kernels, adam(): pl.pallas_call(adam_kernel, out_shape=[jax.ShapeDtypeStruct(a.shape, a.dt...  4.9 us

profile of v2, /device:TPU:0, one launch (start us, length us, event | category | flops | bytes accessed | tf_op | source)
XLA Modules:
  0.0 131.1 jit_solution(14248259182176008441)
XLA Ops:
  0.7 125.3 %shard_map.356 = (bf16[2,128,768]{2,1,0:T(8,128)(2,1)}, f32[2,128,768]{2,1,0:T(8,128)}, f32[2,24,384]{2,1,0:T(8,128)}, f32[2,4,24,384]{3,2,1,0:T(8,128)}, f32[2,...) custom-call(s32[2,4]{1,0:T(2,128)} %lengths.1, bf16[2,128,768]{2,1,0:T(8,128)(2,1)} %tok.1, ...), custom_call_target="tpu_custom_call" | custom-call | flops 12999999488 | bytes 10000000 | tf_op jit(solution)/shard_map/pallas_call | solution.py:765
  126.0 4.9 %shard_map.357 = (bf16[2,128,768]{2,1,0:T(8,128)(2,1)}, f32[2,128,768]{2,1,0:T(8,128)}, f32[24,2304]{1,0:T(8,128)}, f32[24,768]{1,0:T(8,128)}, f32[24,3072]{1,0:...) custom-call(f32[2,24,384]{2,1,0:T(8,128)} %get-tuple-element.47.o0, ...), custom_call_target="tpu_custom_call" | custom-call | tf_op jit(solution)/shard_map/pallas_call | solution.py:849
